TPU v7x, 32 devices: a whole 2x2x4 slice. The times are simulated.
32 devices in a mesh: tok: 4 (over y, x), feat: 8 (over z, core).
Axes of the slice: x: 2, y: 2, z: 4, core: 2. Of those that a mesh axis runs over, the one named last changes fastest.
Arguments:
- tokens: bfloat16 [256, 8192], P('tok', 'feat'), may hold values from -6 to 6
- gain: float32 [8192], replicated, may hold values from 0.1 to 1.9
- proj: bfloat16 [8192, 8192], P('tok', 'feat'), may hold values from -0.0625 to 0.0625
- panel_index: int32 [1], replicated, may hold values from 0 to 31
Outputs:
- panel_rows: float32 [256, 8192], P(None, 'feat')
- solved_cross: float32 [256, 8192], P(None, 'feat')
All inputs are finite; a program needn't handle non-finite values.
Results may differ from a plain program's by a relative error of at most 0.01.
Values may be sent and summed in bfloat16 or wider, within the bound.
A program may use at most 64 MiB of HBM per device.

v0:
```python
import math

import jax
import jax.numpy as jnp
from jax import lax
from jax.sharding import PartitionSpec as P

D = 8192
PANEL = 256


def solve_pair(factor, gram_part, cross_part):
    first = lax.linalg.triangular_solve(factor, gram_part, left_side=True, lower=True)
    second = lax.linalg.triangular_solve(factor, cross_part, left_side=True, lower=True)
    return (first, second)


def body(tokens, gain, proj, panel_index):
    token_full = lax.all_gather(tokens, "feat", axis=1, tiled=True)
    wide_rows = token_full.astype(jnp.float32)
    inv_rms = lax.rsqrt(jnp.mean(wide_rows * wide_rows, axis=1, keepdims=True) + 1e-05)
    normed = (wide_rows * inv_rms * gain[None, :]).astype(jnp.bfloat16)
    local_cols = tokens.shape[1]
    projected = jnp.dot(
        normed, lax.all_gather(proj, "tok", axis=0, tiled=True), preferred_element_type=jnp.float32
    )
    own_values = tokens.astype(jnp.float32)
    outputs = (own_values + projected).astype(jnp.bfloat16)
    change = (outputs.astype(jnp.float32) - own_values).astype(jnp.bfloat16)
    band_start = panel_index[0] * PANEL
    band_cols = lax.dynamic_slice_in_dim(token_full, band_start, PANEL, 1)
    gram_part = jnp.dot(band_cols.T, tokens, preferred_element_type=jnp.float32)
    cross_part = jnp.dot(band_cols.T, change, preferred_element_type=jnp.float32)
    gram_sum, cross_sum = (
        lax.psum_scatter(gram_part, "tok", scatter_dimension=0, tiled=True),
        lax.psum_scatter(cross_part, "tok", scatter_dimension=0, tiled=True),
    )
    tok_count = lax.axis_size("tok")
    feat_count = lax.axis_size("feat")
    token_count = tokens.shape[0] * tok_count
    rows_here = gram_sum.shape[0]
    row_ids = lax.broadcasted_iota(jnp.int32, gram_sum.shape, 0) + lax.axis_index("tok") * rows_here
    col_ids = (
        lax.broadcasted_iota(jnp.int32, gram_sum.shape, 1) + lax.axis_index("feat") * local_cols
    )
    ridge_mask = jnp.where(col_ids == row_ids + band_start, 0.1, 0.0).astype(jnp.float32)
    gram_rows = gram_sum / token_count + ridge_mask
    cross_rows = cross_sum * (math.sqrt(D) / token_count)
    slab_rows = PANEL // feat_count
    own_slab = lax.dynamic_slice_in_dim(band_cols, lax.axis_index("feat") * slab_rows, slab_rows, 1)
    partial_value = jnp.dot(own_slab.T, band_cols, preferred_element_type=jnp.float32)
    summed = lax.psum(partial_value, "tok")
    diag_sum = lax.all_gather(summed, "feat", axis=0, tiled=True)
    diag_block = diag_sum / token_count + 0.1 * jnp.eye(PANEL, dtype=jnp.float32)
    factor = jnp.linalg.cholesky(diag_block)
    gram_some, cross_some = (
        lax.all_to_all(gram_rows, "tok", split_axis=1, concat_axis=0, tiled=True),
        lax.all_to_all(cross_rows, "tok", split_axis=1, concat_axis=0, tiled=True),
    )
    panel_some, solved_some = solve_pair(factor, gram_some, cross_some)
    panel_rows, solved_cross = (
        lax.all_gather(panel_some, "tok", axis=1, tiled=True),
        lax.all_gather(solved_some, "tok", axis=1, tiled=True),
    )
    return (panel_rows, solved_cross)


def solution(mesh):
    return jax.shard_map(
        body,
        mesh=mesh,
        in_specs=(P("tok", "feat"), P(), P("tok", "feat"), P()),
        out_specs=(P(None, "feat"), P(None, "feat")),
        check_vma=False,
    )
```

profile of v0, /device:TPU:13, one launch (start us, length us, event | category | flops | bytes accessed | tf_op | source)
XLA Modules:
  0.0 322.3 jit_solution(10894789533135216207)
XLA Ops:
  9.4 24.1 %all-gather.5.cloned.1.call-done = bf16[64,8192]{1,0:T(8,128)(2,1)} async-done(((bf16[64,1024]{1,0:T(8,128)(2,1)}), bf16[64,8192]{1,0:T(8,128)(2,1)}) %all-gather.5.cloned.1.call-update) | async-done | bytes 1048592 | tf_op jit(solution)/shard_map/all_gather | solution.py:19
  33.5 1.1 fusion.30
  34.6 11.6 %psum.7 = f32[32,256]{1,0:T(8,128)S(1)} all-reduce(f32[32,256]{1,0:T(8,128)S(1)} %fusion.30), channel_id=1, replica_groups=mesh['tok'=4,'feat'=8] {'tok'}, use_global_device_ids=true, to_apply=%region_0.0 | all-reduce | flops 8192 | bytes 65536 | tf_op jit(solution)/shard_map/psum | solution.py:52
  46.2 16.4 %all_gather.16 = f32[256,256]{1,0:T(8,128)S(1)} all-gather(f32[32,256]{1,0:T(8,128)S(1)} %psum.7), channel_id=1, replica_groups=mesh['tok'=4,'feat'=8] {'feat'}, dimensions={0}, use_global_device_ids=true | all-gather | bytes 294912 | tf_op jit(solution)/shard_map/all_gather | solution.py:53
  63.0 11.7 %cholesky.49 = f32[128,128]{1,0:T(8,128)S(1)} custom-call(f32[128,128]{1,0:T(8,128)S(1)} %cholesky.115), custom_call_target="Cholesky" | custom-call | tf_op jit(solution)/shard_map/jit(cholesky)/cholesky | solution.py:55
  74.7 9.8 %custom-call.14 = f32[1,128,128]{1,2,0:T(8,128)S(1)} custom-call(f32[1,128,128]{2,1,0:T(8,128)S(1)} %get-tuple-element.54), custom_call_target="InvertDiagBlocksLowerTriangular" | custom-call | tf_op jit(solution)/shard_map/jit(cholesky)/cholesky | solution.py:55
  84.8 1.3 fusion.28
  86.8 11.7 %cholesky.103 = f32[128,128]{1,0:T(8,128)S(1)} custom-call(f32[128,128]{1,0:T(8,128)S(1)} %convolution_subtract_fusion.2), custom_call_target="Cholesky" | custom-call | tf_op jit(solution)/shard_map/jit(cholesky)/cholesky | solution.py:55
  101.1 90.8 %all-gather.9.cloned.1.call-done = bf16[8192,1024]{1,0:T(8,128)(2,1)} async-done(((bf16[2048,1024]{1,0:T(8,128)(2,1)}), bf16[8192,1024]{1,0:T(8,128)(2,1)}) %all-gather.9.cloned.1.call-update) | async-done | bytes 16777232 | tf_op jit(solution)/shard_map/all_gather | solution.py:25
  191.9 10.1 %fusion.7 = f32[256,1024]{1,0:T(8,128)} fusion(bf16[8192,1024]{1,0:T(8,128)(2,1)} %all-gather.9.cloned.1.call-done, bf16[64,8192]{1,0:T(8,128)(2,1)S(1)} %copy-done, f32[8192]{0:T(1024)S(1)} %copy-done.3, f32[64]{0:T(128)S(1)} %add_rsqrt_fusion, bf16[64,1024]{1,0:T(8,128)(2,1)S(1)} %copy-done.1, s32[]{:T(128)S(6)} %select_n.20), kind=kOutput, calls=%fused_computation.12 | convolution fusion | flops 1109786624 | bytes 19071492 | tf_op jit(solution)/shard_map/dot_general | solution.py:33
  202.0 21.1 %reduce-scatter.3.cloned.1.call-done = f32[64,1024]{1,0:T(8,128)} async-done(((f32[256,1024]{1,0:T(8,128)}), f32[64,1024]{1,0:T(8,128)}) %reduce-scatter.3.cloned.1.call-update) | async-done | bytes 262160 | tf_op jit(solution)/shard_map/reduce_scatter | solution.py:35
  223.1 1.0 select_add_fusion
  224.1 0.7 copy.37
  224.8 3.7 %all-to-all-start = ((f32[64,4,256]{2,0,1:T(8,128)}), f32[64,4,256]{2,0,1:T(8,128)S(1)}, u32[]{:S(2)}, u32[]{:S(2)}) async-start(f32[64,4,256]{2,0,1:T(8,128)} %bitcast.48), calls=%async_computation.1 | async-start | bytes 524288 | tf_op jit(solution)/shard_map/all_to_all | solution.py:57
  228.6 4.0 %while.4 = (s32[]{:T(128)}, f32[256,256]{0,1:T(8,128)S(1)}, s32[2,2]{1,0:T(2,128)S(1)}, f32[2,128,128]{2,1,0:T(8,128)S(1)}, s32[]{:T(128)}) while((s32[]{:T(128)}, f32[256,256]{0,1:T(8,128)S(1)}, s32[2,2]{1,0:T(2,128)S(1)}, f32[2,128,128]{2,1,0:T(8,128)S(1)}, s32[]{:T(128)}) %tuple.36), condition=%wide.while_cond, body=%wide.while_body.sunk | while | flops 2 | bytes 393329 | solution.py:13
  229.2 1.3 dynamic-slice.9
  231.2 1.3 dynamic-slice.9
  232.6 19.7 %custom-call.16 = f32[2,128,128]{1,2,0:T(8,128)S(1)} custom-call(f32[2,128,128]{2,1,0:T(8,128)S(1)} %get-tuple-element.17), custom_call_target="InvertDiagBlocksLowerTriangular" | custom-call | tf_op jit(solution)/shard_map/triangular_solve/custom-call.0 | solution.py:13
  254.5 1.0 broadcast_multiply_fusion
  255.5 7.1 %all_to_all.38 = f32[64,4,256]{2,0,1:T(8,128)S(1)} all-to-all(f32[64,4,256]{2,0,1:T(8,128)S(1)} %bitcast.61), channel_id=1, replica_groups=mesh['tok'=4,'feat'=8] {'tok'}, dimensions={1} | all-to-all | bytes 524288 | tf_op jit(solution)/shard_map/all_to_all | solution.py:58
  264.3 19.0 %all-gather.7.cloned.1.call-done = f32[256,1024]{1,0:T(8,128)} async-done(((f32[256,256]{1,0:T(8,128)}), f32[256,1024]{1,0:T(8,128)}) %all-gather.7.cloned.1.call-update) | async-done | bytes 1048592 | tf_op jit(solution)/shard_map/all_gather | solution.py:62
  283.3 28.8 %all-gather.11.cloned.1.call-done = f32[256,1024]{1,0:T(8,128)} async-done(((f32[256,256]{1,0:T(8,128)}), f32[256,1024]{1,0:T(8,128)}) %all-gather.11.cloned.1.call-update) | async-done | bytes 1048592 | tf_op jit(solution)/shard_map/all_gather | solution.py:63
  312.1 2.4 copy.54
  314.5 1.0 copy.55
  (63 shorter events, 9.3 us)
Async XLA Ops:
  7.2 26.3 %all-gather.5.cloned.1.call-start = ((), (), s32[]{:S(2)}) async-start(), calls=%async_computation.4 | async-start | bytes 1179648 | tf_op jit(solution)/shard_map/all_gather | solution.py:19
  7.9 184.0 %all-gather.9.cloned.1.call-start = ((), (), s32[]{:S(2)}) async-start(), calls=%async_computation.7 | async-start | bytes 20971520 | tf_op jit(solution)/shard_map/all_gather | solution.py:25
  8.6 76.1 %copy-start.1 = (bf16[64,1024]{1,0:T(8,128)(2,1)S(1)}, bf16[64,1024]{1,0:T(8,128)(2,1)}, u32[]{:S(2)}) copy-start(bf16[64,1024]{1,0:T(8,128)(2,1)} %param.6) | copy-start | bytes 393220
  8.7 214.4 %reduce-scatter.3.cloned.1.call-start = ((), (), s32[]{:S(2)}) async-start(), calls=%async_computation.5 | async-start | bytes 1310720 | tf_op jit(solution)/shard_map/reduce_scatter | solution.py:35
  33.5 51.3 %copy-start = (bf16[64,8192]{1,0:T(8,128)(2,1)S(1)}, bf16[64,8192]{1,0:T(8,128)(2,1)}, u32[]{:S(2)}) copy-start(bf16[64,8192]{1,0:T(8,128)(2,1)} %all-gather.5.cloned.1.call-done) | copy-start | bytes 3145732
  84.8 107.1 %copy-start.3 = (f32[8192]{0:T(1024)S(1)}, f32[8192]{0:T(1024)}, u32[]{:S(2)}) copy-start(f32[8192]{0:T(1024)} %param.7) | copy-start | bytes 98308
  86.1 168.3 %reduce-scatter.5.cloned.1.call-start = ((), (), s32[]{:S(2)}) async-start(), calls=%async_computation.8 | async-start | bytes 1310720 | tf_op jit(solution)/shard_map/reduce_scatter | solution.py:36
  224.8 27.5 %all-to-all-start = ((f32[64,4,256]{2,0,1:T(8,128)}), f32[64,4,256]{2,0,1:T(8,128)S(1)}, u32[]{:S(2)}, u32[]{:S(2)}) async-start(f32[64,4,256]{2,0,1:T(8,128)} %bitcast.48), calls=%async_computation.1 | async-start | bytes 524288 | tf_op jit(solution)/shard_map/all_to_all | solution.py:57
  228.6 54.7 %all-gather.7.cloned.1.call-start = ((), (), s32[]{:S(2)}) async-start(), calls=%async_computation.6 | async-start | bytes 1310720 | tf_op jit(solution)/shard_map/all_gather | solution.py:62
  254.0 58.0 %all-gather.11.cloned.1.call-start = ((), (), s32[]{:S(2)}) async-start(), calls=%async_computation.9 | async-start | bytes 1310720 | tf_op jit(solution)/shard_map/all_gather | solution.py:63
  312.1 2.4 copy-start.2
Sparse Core Ops, SparseCore 0:
  9.6 23.8 all-gather.4
  35.3 156.5 all-gather.8
  195.4 27.6 reduce-scatter.2
  226.6 27.7 reduce-scatter.4
  256.7 26.5 all-gather.6
  285.5 26.4 all-gather.10
where the time goes:
time: 324 us; the launch traced here: 322 us
  waiting for transfers between devices  186 us (57%)
  other arithmetic  57.6 us (18%)
  blocking collectives  35.1 us (11%)
  between operations  16.4 us (5%)
  matrix products  14.8 us (5%)
  local copies, waits for them, and re-layouts  8.71 us (3%)
  starting transfers between devices  4.1 us (1%)
    all_gather x1, waiting for transfers between devices, body(): lax.all_gather(proj, 'tok', axis=0, tiled=True)  90.8 us
    another operation x6, other arithmetic, body(): factor = jnp.linalg.cholesky(diag_block)  34 us
    all_gather x1, waiting for transfers between devices, body(): lax.all_gather(solved_some, 'tok', axis=1, tiled=True)  28.8 us
    all_gather x1, waiting for transfers between devices, body(): token_full = lax.all_gather(tokens, 'feat', axis=1, tiled=True)  24.1 us
    reduce_scatter x1, waiting for transfers between devices, body(): lax.psum_scatter(gram_part, 'tok', scatter_dimension=0, tiled=True)  21.1 us
    another operation x5, other arithmetic, solve_pair(): lax.linalg.triangular_solve(factor, gram_part, left_side=True, lower=True)  20.4 us
    all_gather x1, waiting for transfers between devices, body(): lax.all_gather(panel_some, 'tok', axis=1, tiled=True)  19 us
    all_gather x1, blocking collectives, body(): diag_sum = lax.all_gather(summed, 'feat', axis=0, tiled=True)  16.4 us
  transfers between devices with their start and end apart: 7, of which 6 were waited for; matrix products, arithmetic and copies ran while one was open for 24% of the time, Pallas kernels for 0%

commit v1 on v0

--- a/solution.py
+++ b/solution.py
@@ -3,11 +3,337 @@
 import jax
 import jax.numpy as jnp
 from jax import lax
+from jax.experimental import pallas as pl
+from jax.experimental.pallas import tpu as pltpu
 from jax.sharding import PartitionSpec as P
 
 D = 8192
 PANEL = 256
-
+MESH = pl.DeviceIdType.MESH
+HIGH = lax.Precision.HIGHEST
+F32 = jnp.float32
+BF16 = jnp.bfloat16
+STEP = 32
+TILE = 128
+OUTER = PANEL // STEP
+REST = PANEL - STEP
+
+
+def dot0(a, b, precision=None):
+    return lax.dot_general(a, b, (((0,), (0,)), ((), ())), precision=precision, preferred_element_type=F32)
+
+
+def lanes(col):
+    return jnp.broadcast_to(col, (8, TILE))
+
+
+def eliminate(ob, wa, wi):
+    r0 = pl.multiple_of(ob * STEP, STEP)
+    groups = []
+    for g in range(STEP // 8):
+        rows = pl.ds(pl.multiple_of(r0 + 8 * g, 8), 8)
+        groups.append(
+            [wa[rows, 0:128], wa[rows, 128:256], wi[rows, 0:128], wi[rows, 128:256]]
+        )
+    sub = lax.broadcasted_iota(jnp.int32, (8, TILE), 0)
+    n = STEP // 8
+    for k in range(n):
+        cols = {
+            g: [lanes(groups[g][0][:, 8 * k + j : 8 * k + j + 1]) for j in range(8)]
+            for g in range(k, n)
+        }
+        a = [[lanes(cols[k][j][i : i + 1, :]) if j <= i else None for j in range(8)] for i in range(8)]
+        low = [[None] * 8 for _ in range(8)]
+        inv = [None] * 8
+        for j in range(8):
+            inv[j] = lax.rsqrt(a[j][j])
+            for i in range(j + 1, 8):
+                low[i][j] = a[i][j] * inv[j]
+            for l in range(j + 1, 8):
+                for i in range(l, 8):
+                    a[i][l] = a[i][l] - low[i][j] * low[l][j]
+        m = [[None] * 8 for _ in range(8)]
+        for j in range(8):
+            m[j][j] = inv[j]
+            for i in range(j + 1, 8):
+                acc = low[i][j] * m[j][j]
+                for l in range(j + 1, i):
+                    acc = acc + low[i][l] * m[l][j]
+                m[i][j] = -inv[i] * acc
+        zero = jnp.zeros((8, TILE), F32)
+        mcol, mrow = [], []
+        for j in range(8):
+            c = zero
+            for i in range(j, 8):
+                c = jnp.where(sub == i, m[i][j], c)
+            mcol.append(c)
+        for i in range(8):
+            c = zero
+            for j in range(0, i + 1):
+                c = jnp.where(sub == j, m[i][j], c)
+            mrow.append(c)
+        done = []
+        for v in range(4):
+            r = groups[k][v]
+            u = mcol[0] * lanes(r[0:1, :])
+            for j in range(1, 8):
+                u = u + mcol[j] * lanes(r[j : j + 1, :])
+            done.append(u)
+            if k < n - 1:
+                w = mrow[0] * lanes(u[0:1, :])
+                for j in range(1, 8):
+                    w = w + mrow[j] * lanes(u[j : j + 1, :])
+                wb = [lanes(w[j : j + 1, :]) for j in range(8)]
+                for g in range(k + 1, n):
+                    s = cols[g][0] * wb[0]
+                    for j in range(1, 8):
+                        s = s + cols[g][j] * wb[j]
+                    groups[g][v] = groups[g][v] - s
+        groups[k] = done
+    for g in range(n):
+        rows = pl.ds(pl.multiple_of(r0 + 8 * g, 8), 8)
+        wi[rows, 0:128] = groups[g][2]
+        wi[rows, 128:256] = groups[g][3]
+    ua = jnp.concatenate(
+        [jnp.concatenate([groups[g][0] for g in range(n)], axis=0), jnp.concatenate([groups[g][1] for g in range(n)], axis=0)],
+        axis=1,
+    )
+    ui = jnp.concatenate(
+        [jnp.concatenate([groups[g][2] for g in range(n)], axis=0), jnp.concatenate([groups[g][3] for g in range(n)], axis=0)],
+        axis=1,
+    )
+    rest = pl.ds(pl.multiple_of(r0 + STEP, STEP), REST)
+    left = ua[:, STEP:]
+    if STEP % 128:
+        left = pltpu.roll(ua, PANEL - STEP, 1)
+    wa[rest, :] = pltpu.roll(wa[rest, :] - dot0(left, ua, HIGH)[:REST], PANEL - STEP, 1)
+    wi[rest, :] = wi[rest, :] - dot0(left, ui, HIGH)[:REST]
+
+
+def kernel(
+    tcount, fcount, tokens, gain, proj_hbm, slice_ref, rel, panel, solved,
+    proj, bfb, btb, own, zbuf, xbuf, xg, ssb, rsb, rss, agb, wa, wi, accs, inv_ref,
+    proj_sem, bf_s, bf_r, bt_s, bt_r, oc_s, oc_r, a1_s, a1_r, a2_s, a2_r, a3_s, a3_r,
+    ss_s, ss_r, rs_s, rs_r, ag_s, ag_r,
+):
+    t = lax.axis_index("tok")
+    f = lax.axis_index("feat")
+    z, c = f // 2, f % 2
+    sib = f + 1 - 2 * c
+    zcount = fcount // 2
+    rows, cols = tokens.shape
+    total = rows * tcount
+    quarter = cols // tcount
+
+    load = pltpu.make_async_copy(proj_hbm, proj, proj_sem)
+    load.start()
+    barrier = pltpu.get_barrier_semaphore()
+    for d in range(1, fcount):
+        pl.semaphore_signal(barrier, inc=1, device_id=(t, (f + d) % fcount), device_id_type=MESH)
+    for d in range(1, tcount):
+        pl.semaphore_signal(barrier, inc=1, device_id=((t + d) % tcount, f), device_id_type=MESH)
+    bfb[f] = slice_ref[...]
+    own[t] = tokens[...]
+    zbuf[z] = tokens[...]
+    pl.semaphore_wait(barrier, fcount + tcount - 2)
+
+    def to(src, dst, ssem, rsem, device):
+        return pltpu.make_async_remote_copy(
+            src_ref=src, dst_ref=dst, send_sem=ssem, recv_sem=rsem, device_id=device, device_id_type=MESH
+        )
+
+    sent = []
+
+    def send(src, dst, ssem, rsem, device):
+        copy = to(src, dst, ssem, rsem, device)
+        copy.start()
+        sent.append(copy)
+
+    def got(buf, slot, rsem):
+        to(buf.at[slot], buf.at[slot], rsem.at[slot], rsem.at[slot], (t, sib)).wait_recv()
+
+    for d in range(1, fcount):
+        send(bfb.at[f], bfb.at[f], bf_s.at[d], bf_r.at[f], (t, (f + d) % fcount))
+    for d in range(1, tcount):
+        send(own.at[t], own.at[t], oc_s.at[d], oc_r.at[t], ((t + d) % tcount, f))
+    for d in range(1, zcount):
+        send(zbuf.at[z], zbuf.at[z], a1_s.at[d], a1_r.at[z], (t, ((z + d) % zcount) * 2 + c))
+
+    def pass_on(d):
+        zz = (z + d) % zcount
+        if d:
+            got(zbuf, zz, a1_r)
+
+        @pl.when(zz == t)
+        def _():
+            xbuf[c, t] = zbuf[zz]
+
+        @pl.when(zz != t)
+        def _():
+            to(zbuf.at[zz], xbuf.at[c, t], a2_s.at[d], a2_r.at[t], (zz, f)).start()
+
+    def pass_done(d):
+        zz = (z + d) % zcount
+
+        @pl.when(zz != t)
+        def _():
+            to(zbuf.at[zz], xbuf.at[c, t], a2_s.at[d], a2_r.at[t], (zz, f)).wait_send()
+
+    pass_on(0)
+    for d in range(1, fcount):
+        got(bfb, (f + d) % fcount, bf_r)
+    whole = bfb[0].astype(F32)
+    for d in range(1, fcount):
+        whole = whole + bfb[d].astype(F32)
+    btb[t] = whole.astype(BF16)
+    for d in range(1, tcount):
+        send(btb.at[t], btb.at[t], bt_s.at[d], bt_r.at[t], ((t + d) % tcount, f))
+    for d in range(1, tcount):
+        got(btb, (t + d) % tcount, bt_r)
+    band = btb[...].reshape(total, PANEL)
+    eye = (
+        lax.broadcasted_iota(jnp.int32, (PANEL, PANEL), 0) == lax.broadcasted_iota(jnp.int32, (PANEL, PANEL), 1)
+    ).astype(F32)
+    wa[0:PANEL, :] = dot0(band, band) / total + 0.1 * eye
+    wi[0:PANEL, :] = eye
+    wa[PANEL:, :] = jnp.zeros((PANEL, PANEL), F32)
+    wi[PANEL:, :] = jnp.zeros((PANEL, PANEL), F32)
+
+    def chol(lo, hi):
+        @pl.loop(lo, hi)
+        def _(ob):
+            eliminate(ob, wa, wi)
+
+    chol(0, 1)
+    for d in range(1, tcount):
+        got(own, (t + d) % tcount, oc_r)
+    wide = own[...].reshape(total, cols).astype(F32)
+    ssb[f] = lax.dot_general(
+        jnp.ones((8, cols), F32), wide * wide, (((1,), (1,)), ((), ())), precision=HIGH, preferred_element_type=F32
+    )
+    for d in range(1, fcount):
+        send(ssb.at[f], ssb.at[f], ss_s.at[d], ss_r.at[f], (t, (f + d) % fcount))
+    chol(1, 3)
+    pass_on(1)
+    pass_on(3)
+    chol(3, 4)
+    pass_on(2)
+    for d in range(1, fcount):
+        got(ssb, (f + d) % fcount, ss_r)
+    sums = ssb[0]
+    for d in range(1, fcount):
+        sums = sums + ssb[d]
+    inv_row = lax.rsqrt(sums / (cols * fcount) + 1e-05)
+    inv_ref[...] = dot0(inv_row, jnp.full((8, TILE), 0.125, F32), HIGH)
+    chol(4, 6)
+
+    def share(d):
+        tt = (t + d) % tcount
+        if d:
+            to(xbuf.at[c, tt], xbuf.at[c, tt], a2_r.at[tt], a2_r.at[tt], (t, sib)).wait_recv()
+        send(xbuf.at[c, tt], xbuf.at[c, tt], a3_s.at[d], a3_r.at[tt], (t, sib))
+
+    for d in range(tcount):
+        share(d)
+    width = 2 * cols
+
+    def scaled(half):
+        g = gain[:, pl.ds(pl.multiple_of(t * width + half * cols, cols), cols)]
+        xg[half] = (xbuf[half].reshape(total, cols).astype(F32) * g).astype(BF16)
+
+    scaled(c)
+    for d in range(tcount):
+        tt = (t + d) % tcount
+        to(xbuf.at[1 - c, tt], xbuf.at[1 - c, tt], a3_r.at[tt], a3_r.at[tt], (t, sib)).wait_recv()
+    scaled(1 - c)
+    load.wait()
+    for d in list(range(1, tcount)) + [0]:
+        q = (t + d) % tcount
+        at = pl.ds(pl.multiple_of(q * quarter, quarter), quarter)
+        part = jnp.dot(xg[0], proj[0:cols, at], preferred_element_type=F32)
+        part = part + jnp.dot(xg[1], proj[cols : 2 * cols, at], preferred_element_type=F32)
+        if d:
+            rss[q] = part.astype(BF16)
+            send(rss.at[q], rsb.at[t], rs_s.at[d], rs_r.at[t], (q, f))
+        else:
+            accs[...] = part
+    chol(6, OUTER)
+    linv = wi[0:PANEL, :]
+    for d in range(1, tcount):
+        got(rsb, (t + d) % tcount, rs_r)
+    acc = accs[...]
+    for d in range(1, tcount):
+        acc = acc + rsb[(t + d) % tcount].astype(F32)
+    inv2 = jnp.concatenate([inv_ref[...]] * (quarter // TILE), axis=1)
+    mine = own[:, :, pl.ds(pl.multiple_of(t * quarter, quarter), quarter)].reshape(total, quarter).astype(F32)
+    out = (mine + acc * inv2).astype(BF16)
+    change = (out.astype(F32) - mine).astype(BF16)
+    band = btb[...].reshape(total, PANEL)
+    cross = dot0(band, change) * (math.sqrt(D) / total)
+    result = jnp.dot(linv, cross, precision=HIGH, preferred_element_type=F32)
+    agb[t] = result.astype(BF16)
+    for d in range(1, tcount):
+        send(agb.at[t], agb.at[t], ag_s.at[d], ag_r.at[t], ((t + d) % tcount, f))
+    shape = (PANEL, quarter)
+    for q in range(tcount):
+        at = slice(q * quarter, (q + 1) * quarter)
+        gram = dot0(band, own[:, :, at].reshape(total, quarter)) / total
+        row_ids = lax.broadcasted_iota(jnp.int32, shape, 0)
+        col_ids = jnp.broadcast_to(rel[:, at], shape)
+        gram = gram + jnp.where(col_ids == row_ids, 0.1, 0.0).astype(F32)
+        panel[:, at] = jnp.dot(linv, gram, precision=HIGH, preferred_element_type=F32)
+    solved[:, pl.ds(pl.multiple_of(t * quarter, quarter), quarter)] = result
+    for d in range(1, tcount):
+        q = (t + d) % tcount
+        got(agb, q, ag_r)
+        solved[:, pl.ds(pl.multiple_of(q * quarter, quarter), quarter)] = agb[q].astype(F32)
+    for copy in sent:
+        copy.wait_send()
+    for d in range(zcount):
+        pass_done(d)
+
+
+def fused(tcount, fcount, tokens, gain, proj, panel_index):
+    rows, cols = tokens.shape
+    total, quarter, zcount = rows * tcount, cols // tcount, fcount // 2
+    start = panel_index[0] * PANEL
+    f = lax.axis_index("feat")
+    band_slice = lax.dynamic_slice_in_dim(tokens, start % cols, PANEL, 1)
+    band_slice = jnp.where(start // cols == f, band_slice, jnp.zeros_like(band_slice))
+    rel = (lax.broadcasted_iota(jnp.int32, (1, cols), 1) + (f * cols - start)).astype(jnp.int32)
+    vmem = pl.BlockSpec(memory_space=pltpu.VMEM)
+    dma = lambda n: pltpu.SemaphoreType.DMA((n,))
+    scratch = [
+        pltpu.VMEM(proj.shape, BF16),
+        pltpu.VMEM((fcount, rows, PANEL), BF16),
+        pltpu.VMEM((tcount, rows, PANEL), BF16),
+        pltpu.VMEM((tcount, rows, cols), BF16),
+        pltpu.VMEM((zcount, rows, cols), BF16),
+        pltpu.VMEM((2, tcount, rows, cols), BF16),
+        pltpu.VMEM((2, total, cols), BF16),
+        pltpu.VMEM((fcount, 8, total), F32),
+        pltpu.VMEM((tcount, total, quarter), BF16),
+        pltpu.VMEM((tcount, total, quarter), BF16),
+        pltpu.VMEM((tcount, PANEL, quarter), BF16),
+        pltpu.VMEM((2 * PANEL, PANEL), F32),
+        pltpu.VMEM((2 * PANEL, PANEL), F32),
+        pltpu.VMEM((total, quarter), F32),
+        pltpu.VMEM((total, TILE), F32),
+        pltpu.SemaphoreType.DMA,
+    ]
+    for n in (fcount, tcount, tcount, zcount, tcount, tcount, fcount, tcount, tcount):
+        scratch += [dma(n), dma(n)]
+    out = jax.ShapeDtypeStruct((PANEL, cols), F32)
+    return pl.pallas_call(
+        lambda *refs: kernel(tcount, fcount, *refs),
+        out_shape=(out, out),
+        in_specs=[vmem, vmem, pl.BlockSpec(memory_space=pl.ANY), vmem, vmem],
+        out_specs=(vmem, vmem),
+        scratch_shapes=scratch,
+        compiler_params=pltpu.CompilerParams(
+            collective_id=0, has_side_effects=True, vmem_limit_bytes=48 * 1024 * 1024
+        ),
+    )(tokens, gain[None, :], proj, band_slice, rel)
 
 def solve_pair(factor, gram_part, cross_part):
     first = lax.linalg.triangular_solve(factor, gram_part, left_side=True, lower=True)
@@ -15,7 +341,7 @@
     return (first, second)
 
 
-def body(tokens, gain, proj, panel_index):
+def general(tokens, gain, proj, panel_index):
     token_full = lax.all_gather(tokens, "feat", axis=1, tiled=True)
     wide_rows = token_full.astype(jnp.float32)
     inv_rms = lax.rsqrt(jnp.mean(wide_rows * wide_rows, axis=1, keepdims=True) + 1e-05)
@@ -66,6 +392,22 @@
 
 
 def solution(mesh):
+    tcount, fcount = mesh.shape["tok"], mesh.shape["feat"]
+
+    def body(tokens, gain, proj, panel_index):
+        rows, cols = tokens.shape
+        fits = (
+            fcount == 2 * tcount
+            and proj.shape[0] == 2 * cols
+            and rows % 16 == 0
+            and rows * tcount == PANEL
+            and cols % (tcount * TILE) == 0
+            and cols % PANEL == 0
+        )
+        if fits:
+            return fused(tcount, fcount, tokens, gain, proj, panel_index)
+        return general(tokens, gain, proj, panel_index)
+
     return jax.shard_map(
         body,
         mesh=mesh,

time: 324 us -> 61.1 us (0.19)
  the two profiles are of different devices: /device:TPU:13 before, /device:TPU:8 now
where the time goes in v1:
time: 61.1 us; the launch traced here: 60.9 us
  Pallas kernels  55 us (90%)
  local copies, waits for them, and re-layouts  3.6 us (6%)
  between operations  1.34 us (2%)
  other arithmetic  0.9 us (1%)
    pallas_call x1, Pallas kernels, fused(): pl.pallas_call(lambda *refs: kernel(tcount, fcount, *refs), out_shape=(ou...  55 us
    unnamed x6, local copies, waits for them, and re-layouts  3.6 us

profile of v1, /device:TPU:8, one launch (start us, length us, event | category | flops | bytes accessed | tf_op | source)
XLA Modules:
  0.0 60.9 jit_solution(381600761990818751)
XLA Ops:
  1.3 0.9 %dynamic-slice_select_fusion.refs_3_ = bf16[64,256]{1,0:T(8,128)(2,1)S(1)} fusion(bf16[64,1024]{1,0:T(8,128)(2,1)} %refs_0_.1, s32[]{:T(128)S(6)} %select_n.25, pred[]{:T(512)S(6)} %eq.5), kind=kLoop, calls=%fused_computation | loop fusion | flops 16384 | bytes 65541 | tf_op jit(solution)/shard_map/jit(_where)/select_n | solution.py:302
  2.2 0.0 copy-start
  2.2 0.9 %copy-done = bf16[64,1024]{1,0:T(8,128)(2,1)S(1)} copy-done((bf16[64,1024]{1,0:T(8,128)(2,1)S(1)}, bf16[64,1024]{1,0:T(8,128)(2,1)}, u32[]{:S(2)}) %copy-start) | copy-done | bytes 131096
  3.1 0.0 copy-start.1
  3.1 0.8 %copy-done.1 = f32[8192]{0:T(1024)S(1)} copy-done((f32[8192]{0:T(1024)S(1)}, f32[8192]{0:T(1024)}, u32[]{:S(2)}) %copy-start.1) | copy-done | bytes 32792
  3.9 55.0 %shard_map.59 = (f32[256,1024]{1,0:T(8,128)S(1)}, f32[256,1024]{1,0:T(8,128)S(1)}) custom-call(bf16[64,1024]{1,0:T(8,128)(2,1)S(1)} %copy-done, f32[1,8192]{1,0:T(1,128)S(1)} %bitcast.2, bf16[2048,1024]{1,0:T(8,128)(2,1)} %refs_2_.1, bf16[64,256]{1,0:T(8,128)(2,1)S(1)} %dynamic-slice_select_fusion.refs_3_, s32[1,1024]{1,0:T(1,128)S(1)} %iota_add_fusion.refs_4_), custom_call_target="tpu_custom_call" | custom-call | tf_op jit(solution)/shard_map/pallas_call | solution.py:327
  58.9 1.0 %copy.9 = f32[256,1024]{1,0:T(8,128)} copy(f32[256,1024]{1,0:T(8,128)S(1)} %get-tuple-element.4) | data formatting | bytes 2097152
  59.9 1.0 %copy.10 = f32[256,1024]{1,0:T(8,128)} copy(f32[256,1024]{1,0:T(8,128)S(1)} %get-tuple-element.5) | data formatting | bytes 2097152
  (1 shorter events, 0.0 us)
Async XLA Ops:
  2.2 0.9 %copy-start = (bf16[64,1024]{1,0:T(8,128)(2,1)S(1)}, bf16[64,1024]{1,0:T(8,128)(2,1)}, u32[]{:S(2)}) copy-start(bf16[64,1024]{1,0:T(8,128)(2,1)} %refs_0_.1) | copy-start | bytes 393220
  3.1 0.8 %copy-start.1 = (f32[8192]{0:T(1024)S(1)}, f32[8192]{0:T(1024)}, u32[]{:S(2)}) copy-start(f32[8192]{0:T(1024)} %param.5) | copy-start | bytes 98308

commit v2 on v1

--- a/solution.py
+++ b/solution.py
@@ -111,9 +111,9 @@
 
 
 def kernel(
-    tcount, fcount, tokens, gain, proj_hbm, slice_ref, rel, panel, solved,
-    proj, bfb, btb, own, zbuf, xbuf, xg, ssb, rsb, rss, agb, wa, wi, accs, inv_ref,
-    proj_sem, bf_s, bf_r, bt_s, bt_r, oc_s, oc_r, a1_s, a1_r, a2_s, a2_r, a3_s, a3_r,
+    tcount, fcount, tokens, gain_hbm, proj_hbm, pidx, panel, solved,
+    proj, gain, bfb, btb, own, zbuf, xbuf, xg, ssb, rsb, rss, agb, wa, wi, accs, inv_ref,
+    proj_sem, gain_sem, own_sem, z_sem, bf_s, bf_r, bt_s, bt_r, oc_s, oc_r, a1_s, a1_r, a2_s, a2_r, a3_s, a3_r,
     ss_s, ss_r, rs_s, rs_r, ag_s, ag_r,
 ):
     t = lax.axis_index("tok")
@@ -126,15 +126,25 @@
     quarter = cols // tcount
 
     load = pltpu.make_async_copy(proj_hbm, proj, proj_sem)
+    start = pidx[0] * PANEL
+    load_own = pltpu.make_async_copy(tokens, own.at[t], own_sem)
+    load_own.start()
+    load_z = pltpu.make_async_copy(tokens, zbuf.at[z], z_sem)
+    load_z.start()
+    load_gain = pltpu.make_async_copy(gain_hbm, gain, gain_sem)
+    load_gain.start()
     load.start()
     barrier = pltpu.get_barrier_semaphore()
     for d in range(1, fcount):
         pl.semaphore_signal(barrier, inc=1, device_id=(t, (f + d) % fcount), device_id_type=MESH)
     for d in range(1, tcount):
         pl.semaphore_signal(barrier, inc=1, device_id=((t + d) % tcount, f), device_id_type=MESH)
-    bfb[f] = slice_ref[...]
-    own[t] = tokens[...]
-    zbuf[z] = tokens[...]
+    shape = (cols, PANEL)
+    pick = lax.broadcasted_iota(jnp.int32, shape, 0) + f * cols == lax.broadcasted_iota(jnp.int32, shape, 1) + start
+    pick = jnp.where(pick, 1.0, 0.0).astype(BF16)
+    load_own.wait()
+    bfb[f] = jnp.dot(own[t], pick, preferred_element_type=F32).astype(BF16)
+    load_z.wait()
     pl.semaphore_wait(barrier, fcount + tcount - 2)
 
     def to(src, dst, ssem, rsem, device):
@@ -180,6 +190,12 @@
             to(zbuf.at[zz], xbuf.at[c, t], a2_s.at[d], a2_r.at[t], (zz, f)).wait_send()
 
     pass_on(0)
+    def share(d):
+        tt = (t + d) % tcount
+        if d:
+            to(xbuf.at[c, tt], xbuf.at[c, tt], a2_r.at[tt], a2_r.at[tt], (t, sib)).wait_recv()
+        send(xbuf.at[c, tt], xbuf.at[c, tt], a3_s.at[d], a3_r.at[tt], (t, sib))
+
     for d in range(1, fcount):
         got(bfb, (f + d) % fcount, bf_r)
     whole = bfb[0].astype(F32)
@@ -188,6 +204,8 @@
     btb[t] = whole.astype(BF16)
     for d in range(1, tcount):
         send(btb.at[t], btb.at[t], bt_s.at[d], bt_r.at[t], ((t + d) % tcount, f))
+    pass_on(1)
+    pass_on(3)
     for d in range(1, tcount):
         got(btb, (t + d) % tcount, bt_r)
     band = btb[...].reshape(total, PANEL)
@@ -205,42 +223,32 @@
             eliminate(ob, wa, wi)
 
     chol(0, 1)
+    pass_on(2)
     for d in range(1, tcount):
         got(own, (t + d) % tcount, oc_r)
     wide = own[...].reshape(total, cols).astype(F32)
+    wide = wide * wide
+    fold = wide[:, 0:TILE]
+    for v in range(1, cols // TILE):
+        fold = fold + wide[:, v * TILE : (v + 1) * TILE]
     ssb[f] = lax.dot_general(
-        jnp.ones((8, cols), F32), wide * wide, (((1,), (1,)), ((), ())), precision=HIGH, preferred_element_type=F32
+        jnp.ones((8, TILE), F32), fold, (((1,), (1,)), ((), ())), precision=HIGH, preferred_element_type=F32
     )
     for d in range(1, fcount):
         send(ssb.at[f], ssb.at[f], ss_s.at[d], ss_r.at[f], (t, (f + d) % fcount))
     chol(1, 3)
-    pass_on(1)
-    pass_on(3)
-    chol(3, 4)
-    pass_on(2)
-    for d in range(1, fcount):
-        got(ssb, (f + d) % fcount, ss_r)
-    sums = ssb[0]
-    for d in range(1, fcount):
-        sums = sums + ssb[d]
-    inv_row = lax.rsqrt(sums / (cols * fcount) + 1e-05)
-    inv_ref[...] = dot0(inv_row, jnp.full((8, TILE), 0.125, F32), HIGH)
-    chol(4, 6)
-
-    def share(d):
-        tt = (t + d) % tcount
-        if d:
-            to(xbuf.at[c, tt], xbuf.at[c, tt], a2_r.at[tt], a2_r.at[tt], (t, sib)).wait_recv()
-        send(xbuf.at[c, tt], xbuf.at[c, tt], a3_s.at[d], a3_r.at[tt], (t, sib))
-
-    for d in range(tcount):
-        share(d)
+    share(0)
+    share(1)
+    share(3)
+    share(2)
+
     width = 2 * cols
 
     def scaled(half):
         g = gain[:, pl.ds(pl.multiple_of(t * width + half * cols, cols), cols)]
         xg[half] = (xbuf[half].reshape(total, cols).astype(F32) * g).astype(BF16)
 
+    load_gain.wait()
     scaled(c)
     for d in range(tcount):
         tt = (t + d) % tcount
@@ -257,7 +265,14 @@
             send(rss.at[q], rsb.at[t], rs_s.at[d], rs_r.at[t], (q, f))
         else:
             accs[...] = part
-    chol(6, OUTER)
+    for d in range(1, fcount):
+        got(ssb, (f + d) % fcount, ss_r)
+    sums = ssb[0]
+    for d in range(1, fcount):
+        sums = sums + ssb[d]
+    inv_row = lax.rsqrt(sums / (cols * fcount) + 1e-05)
+    inv_ref[...] = dot0(inv_row, jnp.full((8, TILE), 0.125, F32), HIGH)
+    chol(3, OUTER)
     linv = wi[0:PANEL, :]
     for d in range(1, tcount):
         got(rsb, (t + d) % tcount, rs_r)
@@ -279,8 +294,8 @@
         at = slice(q * quarter, (q + 1) * quarter)
         gram = dot0(band, own[:, :, at].reshape(total, quarter)) / total
         row_ids = lax.broadcasted_iota(jnp.int32, shape, 0)
-        col_ids = jnp.broadcast_to(rel[:, at], shape)
-        gram = gram + jnp.where(col_ids == row_ids, 0.1, 0.0).astype(F32)
+        col_ids = lax.broadcasted_iota(jnp.int32, shape, 1) + (f * cols + q * quarter)
+        gram = gram + jnp.where(col_ids == row_ids + start, 0.1, 0.0).astype(F32)
         panel[:, at] = jnp.dot(linv, gram, precision=HIGH, preferred_element_type=F32)
     solved[:, pl.ds(pl.multiple_of(t * quarter, quarter), quarter)] = result
     for d in range(1, tcount):
@@ -296,15 +311,11 @@
 def fused(tcount, fcount, tokens, gain, proj, panel_index):
     rows, cols = tokens.shape
     total, quarter, zcount = rows * tcount, cols // tcount, fcount // 2
-    start = panel_index[0] * PANEL
-    f = lax.axis_index("feat")
-    band_slice = lax.dynamic_slice_in_dim(tokens, start % cols, PANEL, 1)
-    band_slice = jnp.where(start // cols == f, band_slice, jnp.zeros_like(band_slice))
-    rel = (lax.broadcasted_iota(jnp.int32, (1, cols), 1) + (f * cols - start)).astype(jnp.int32)
     vmem = pl.BlockSpec(memory_space=pltpu.VMEM)
     dma = lambda n: pltpu.SemaphoreType.DMA((n,))
     scratch = [
         pltpu.VMEM(proj.shape, BF16),
+        pltpu.VMEM((1, gain.shape[0]), F32),
         pltpu.VMEM((fcount, rows, PANEL), BF16),
         pltpu.VMEM((tcount, rows, PANEL), BF16),
         pltpu.VMEM((tcount, rows, cols), BF16),
@@ -320,6 +331,9 @@
         pltpu.VMEM((total, quarter), F32),
         pltpu.VMEM((total, TILE), F32),
         pltpu.SemaphoreType.DMA,
+        pltpu.SemaphoreType.DMA,
+        pltpu.SemaphoreType.DMA,
+        pltpu.SemaphoreType.DMA,
     ]
     for n in (fcount, tcount, tcount, zcount, tcount, tcount, fcount, tcount, tcount):
         scratch += [dma(n), dma(n)]
@@ -327,13 +341,13 @@
     return pl.pallas_call(
         lambda *refs: kernel(tcount, fcount, *refs),
         out_shape=(out, out),
-        in_specs=[vmem, vmem, pl.BlockSpec(memory_space=pl.ANY), vmem, vmem],
+        in_specs=[pl.BlockSpec(memory_space=pl.ANY)] * 3 + [pl.BlockSpec(memory_space=pltpu.SMEM)],
         out_specs=(vmem, vmem),
         scratch_shapes=scratch,
         compiler_params=pltpu.CompilerParams(
             collective_id=0, has_side_effects=True, vmem_limit_bytes=48 * 1024 * 1024
         ),
-    )(tokens, gain[None, :], proj, band_slice, rel)
+    )(tokens, gain[None, :], proj, panel_index)
 
 def solve_pair(factor, gram_part, cross_part):
     first = lax.linalg.triangular_solve(factor, gram_part, left_side=True, lower=True)

time: 61.1 us -> 57.2 us (0.936)
  the two profiles are of different devices: /device:TPU:8 before, /device:TPU:13 now
where the time goes in v2:
time: 57.2 us; the launch traced here: 57 us
  Pallas kernels  52.1 us (91%)
  local copies, waits for them, and re-layouts  3.6 us (6%)
  between operations  1.29 us (2%)
    pallas_call x1, Pallas kernels, fused(): pl.pallas_call(lambda *refs: kernel(tcount, fcount, *refs), out_shape=(ou...  52.1 us
    unnamed x6, local copies, waits for them, and re-layouts  3.6 us

profile of v2, /device:TPU:13, one launch (start us, length us, event | category | flops | bytes accessed | tf_op | source)
XLA Modules:
  0.0 57.0 jit_solution(8169312116494900522)
XLA Ops:
  1.3 0.0 copy-start
  1.3 0.9 %copy-done = bf16[64,1024]{1,0:T(8,128)(2,1)S(1)} copy-done((bf16[64,1024]{1,0:T(8,128)(2,1)S(1)}, bf16[64,1024]{1,0:T(8,128)(2,1)}, u32[]{:S(2)}) %copy-start) | copy-done | bytes 131096
  2.2 0.0 copy-start.1
  2.2 0.8 %copy-done.1 = f32[8192]{0:T(1024)S(1)} copy-done((f32[8192]{0:T(1024)S(1)}, f32[8192]{0:T(1024)}, u32[]{:S(2)}) %copy-start.1) | copy-done | bytes 32792
  2.9 52.1 %shard_map.59 = (f32[256,1024]{1,0:T(8,128)S(1)}, f32[256,1024]{1,0:T(8,128)S(1)}) custom-call(bf16[64,1024]{1,0:T(8,128)(2,1)S(1)} %copy-done, f32[1,8192]{1,0:T(1,128)S(1)} %bitcast.1, bf16[2048,1024]{1,0:T(8,128)(2,1)} %refs_2_.1, s32[1]{0:T(128)S(6)} %copy.8.refs_3_), custom_call_target="tpu_custom_call" | custom-call | tf_op jit(solution)/shard_map/pallas_call | solution.py:341
  55.0 1.0 %copy.9 = f32[256,1024]{1,0:T(8,128)} copy(f32[256,1024]{1,0:T(8,128)S(1)} %get-tuple-element.4) | data formatting | bytes 2097152
  56.0 1.0 %copy.10 = f32[256,1024]{1,0:T(8,128)} copy(f32[256,1024]{1,0:T(8,128)S(1)} %get-tuple-element.5) | data formatting | bytes 2097152
Async XLA Ops:
  1.3 0.9 %copy-start = (bf16[64,1024]{1,0:T(8,128)(2,1)S(1)}, bf16[64,1024]{1,0:T(8,128)(2,1)}, u32[]{:S(2)}) copy-start(bf16[64,1024]{1,0:T(8,128)(2,1)} %refs_0_.1) | copy-start | bytes 393220
  2.2 0.8 %copy-start.1 = (f32[8192]{0:T(1024)S(1)}, f32[8192]{0:T(1024)}, u32[]{:S(2)}) copy-start(f32[8192]{0:T(1024)} %param.5) | copy-start | bytes 98308

commit v3 on v2

--- a/solution.py
+++ b/solution.py
@@ -345,7 +345,7 @@
         out_specs=(vmem, vmem),
         scratch_shapes=scratch,
         compiler_params=pltpu.CompilerParams(
-            collective_id=0, has_side_effects=True, vmem_limit_bytes=48 * 1024 * 1024
+            collective_id=0, has_side_effects=True, vmem_limit_bytes=62 * 1024 * 1024
         ),
     )(tokens, gain[None, :], proj, panel_index)
 

time: 57.2 us -> 59.2 us (1.035)
  local copies, waits for them, and re-layouts: 3.6 us -> 4.61 us
  Pallas kernels: 52.1 us -> 53.1 us
    pallas_call x1, Pallas kernels: 52.1 us -> 53.1 us  [fused(): pl.pallas_call(lambda *refs: kernel(tcount, fcount, *refs), out_shape=(ou...]
    unnamed x6 -> x2, local copies, waits for them, and re-layouts: 3.6 us -> 4.61 us
where the time goes in v3:
time: 59.2 us; the launch traced here: 59 us
  Pallas kernels  53.1 us (90%)
  local copies, waits for them, and re-layouts  4.61 us (8%)
  between operations  1.29 us (2%)
    pallas_call x1, Pallas kernels, fused(): pl.pallas_call(lambda *refs: kernel(tcount, fcount, *refs), out_shape=(ou...  53.1 us
    unnamed x2, local copies, waits for them, and re-layouts  4.61 us

profile of v3, /device:TPU:13, one launch (start us, length us, event | category | flops | bytes accessed | tf_op | source)
XLA Modules:
  0.0 59.0 jit_solution(17653795847330477237)
XLA Ops:
  1.3 53.1 %shard_map.59 = (f32[256,1024]{1,0:T(8,128)}, f32[256,1024]{1,0:T(8,128)}) custom-call(bf16[64,1024]{1,0:T(8,128)(2,1)} %refs_0_.1, f32[1,8192]{1,0:T(1,128)} %bitcast.1, bf16[2048,1024]{1,0:T(8,128)(2,1)} %refs_2_.1, s32[1]{0:T(128)S(6)} %copy.8.refs_3_), custom_call_target="tpu_custom_call" | custom-call | tf_op jit(solution)/shard_map/pallas_call | solution.py:341
  54.4 2.3 %copy.9 = f32[256,1024]{1,0:T(8,128)} copy(f32[256,1024]{1,0:T(8,128)} %get-tuple-element.4) | data formatting | bytes 2097152
  56.7 2.3 %copy.10 = f32[256,1024]{1,0:T(8,128)} copy(f32[256,1024]{1,0:T(8,128)} %get-tuple-element.5) | data formatting | bytes 2097152

commit v4 on v2

--- a/solution.py
+++ b/solution.py
@@ -236,7 +236,7 @@
     )
     for d in range(1, fcount):
         send(ssb.at[f], ssb.at[f], ss_s.at[d], ss_r.at[f], (t, (f + d) % fcount))
-    chol(1, 3)
+    chol(1, 4)
     share(0)
     share(1)
     share(3)
@@ -272,7 +272,7 @@
         sums = sums + ssb[d]
     inv_row = lax.rsqrt(sums / (cols * fcount) + 1e-05)
     inv_ref[...] = dot0(inv_row, jnp.full((8, TILE), 0.125, F32), HIGH)
-    chol(3, OUTER)
+    chol(4, OUTER)
     linv = wi[0:PANEL, :]
     for d in range(1, tcount):
         got(rsb, (t + d) % tcount, rs_r)

time: 57.2 us -> 55.6 us (0.972)
  Pallas kernels: 52.1 us -> 50.5 us
    pallas_call x1, Pallas kernels: 52.1 us -> 50.5 us  [fused(): pl.pallas_call(lambda *refs: kernel(tcount, fcount, *refs), out_shape=(ou...]
where the time goes in v4:
time: 55.6 us; the launch traced here: 55.4 us
  Pallas kernels  50.5 us (91%)
  local copies, waits for them, and re-layouts  3.6 us (6%)
  between operations  1.29 us (2%)
    pallas_call x1, Pallas kernels, fused(): pl.pallas_call(lambda *refs: kernel(tcount, fcount, *refs), out_shape=(ou...  50.5 us
    unnamed x6, local copies, waits for them, and re-layouts  3.6 us

profile of v4, /device:TPU:13, one launch (start us, length us, event | category | flops | bytes accessed | tf_op | source)
XLA Modules:
  0.0 55.4 jit_solution(13088981905161699367)
XLA Ops:
  1.3 0.0 copy-start
  1.3 0.9 %copy-done = bf16[64,1024]{1,0:T(8,128)(2,1)S(1)} copy-done((bf16[64,1024]{1,0:T(8,128)(2,1)S(1)}, bf16[64,1024]{1,0:T(8,128)(2,1)}, u32[]{:S(2)}) %copy-start) | copy-done | bytes 131096
  2.2 0.0 copy-start.1
  2.2 0.8 %copy-done.1 = f32[8192]{0:T(1024)S(1)} copy-done((f32[8192]{0:T(1024)S(1)}, f32[8192]{0:T(1024)}, u32[]{:S(2)}) %copy-start.1) | copy-done | bytes 32792
  2.9 50.5 %shard_map.59 = (f32[256,1024]{1,0:T(8,128)S(1)}, f32[256,1024]{1,0:T(8,128)S(1)}) custom-call(bf16[64,1024]{1,0:T(8,128)(2,1)S(1)} %copy-done, f32[1,8192]{1,0:T(1,128)S(1)} %bitcast.1, bf16[2048,1024]{1,0:T(8,128)(2,1)} %refs_2_.1, s32[1]{0:T(128)S(6)} %copy.8.refs_3_), custom_call_target="tpu_custom_call" | custom-call | tf_op jit(solution)/shard_map/pallas_call | solution.py:341
  53.4 1.0 %copy.9 = f32[256,1024]{1,0:T(8,128)} copy(f32[256,1024]{1,0:T(8,128)S(1)} %get-tuple-element.4) | data formatting | bytes 2097152
  54.4 1.0 %copy.10 = f32[256,1024]{1,0:T(8,128)} copy(f32[256,1024]{1,0:T(8,128)S(1)} %get-tuple-element.5) | data formatting | bytes 2097152
Async XLA Ops:
  1.3 0.9 %copy-start = (bf16[64,1024]{1,0:T(8,128)(2,1)S(1)}, bf16[64,1024]{1,0:T(8,128)(2,1)}, u32[]{:S(2)}) copy-start(bf16[64,1024]{1,0:T(8,128)(2,1)} %refs_0_.1) | copy-start | bytes 393220
  2.2 0.8 %copy-start.1 = (f32[8192]{0:T(1024)S(1)}, f32[8192]{0:T(1024)}, u32[]{:S(2)}) copy-start(f32[8192]{0:T(1024)} %param.5) | copy-start | bytes 98308
